TPU v7x, 256 devices: a whole 4x4x8 slice. The times are simulated.
256 devices in a mesh: blk: 64 (over z, x, core), rep: 4 (over y).
Axes of the slice: x: 4, y: 4, z: 8, core: 2. Of those that a mesh axis runs over, the one named last changes fastest.
Arguments:
- embeddings: float32 [192, 1024, 1024], P('blk')
- pairs: int32 [192, 6], P('blk'), may hold values from 0 to 1, as said below
Outputs:
- best: float32 [192, 1024], P('blk')
Inputs may be any that keep to these rules, and one draw needn't show every extreme that they name: pairs[i, k - 1] is 0 where i + k >= 192; some block lies in no listed pair.
All inputs are finite; a program needn't handle non-finite values.
Results may differ from a plain program's by a relative error of at most 0.0003.
Values may be sent and summed in bfloat16 or wider, within the bound.
A program may use at most 128 MiB of HBM per device.

v0:
```python
import jax
import jax.numpy as jnp
from jax import lax
from jax.sharding import PartitionSpec as P


def from_behind(block, axis, distance):
    devices = range(lax.axis_size(axis))
    route = [(i - distance, i) for i in devices if i - distance in devices]
    return lax.ppermute(block, axis, route)


def per_device(embeddings, pairs):
    blk_dev, rows, width = embeddings.shape
    reach = pairs.shape[1]
    rep_count = lax.axis_size("rep")
    rep_place = lax.axis_index("rep")
    blk_place = lax.axis_index("blk")
    squares = jnp.sum(embeddings * embeddings, axis=2, keepdims=True)
    unit = (embeddings / jnp.sqrt(squares + 1e-06)).astype(jnp.bfloat16)
    pieces = [unit]
    for hop in range(1, reach // blk_dev + 1):
        moved = from_behind(unit, "blk", -hop)
        pieces.append(moved)
    window = jnp.concatenate(pieces, axis=0)
    slots = blk_dev * reach
    listed = pairs.reshape(slots)
    slot_ids = jnp.arange(slots, dtype=jnp.int32)
    mine = jnp.logical_and(listed == 1, slot_ids % reach % rep_count == rep_place)
    count = jnp.sum(mine.astype(jnp.int32))
    ordering = jnp.argsort(jnp.where(mine, slot_ids, slot_ids + slots))
    start = jnp.full((window.shape[0], rows), -1.0, jnp.float32)

    def visit(step, maxima):
        chosen = ordering[step]
        first = chosen // reach
        second = first + chosen % reach + 1
        left = lax.dynamic_index_in_dim(window, first, 0, keepdims=False)
        right = lax.dynamic_index_in_dim(window, second, 0, keepdims=False)
        sim = lax.dot_general(
            left, right, (((1,), (1,)), ((), ())), preferred_element_type=jnp.float32
        )
        row_old = lax.dynamic_index_in_dim(maxima, first, 0, keepdims=True)
        maxima = lax.dynamic_update_index_in_dim(
            maxima, jnp.maximum(row_old, jnp.max(sim, axis=1)[None, :]), first, 0
        )
        col_old = lax.dynamic_index_in_dim(maxima, second, 0, keepdims=True)
        return lax.dynamic_update_index_in_dim(
            maxima, jnp.maximum(col_old, jnp.max(sim, axis=0)[None, :]), second, 0
        )

    maxima = lax.fori_loop(0, count, visit, start)
    gathered_best = maxima[:blk_dev]
    for hop in range(1, reach // blk_dev + 1):
        returned = from_behind(maxima[hop * blk_dev : (hop + 1) * blk_dev], "blk", hop)
        returned = jnp.where(blk_place >= hop, returned, -1.0)
        gathered_best = jnp.maximum(gathered_best, returned)
    return lax.pmax(gathered_best, "rep")


def solution(mesh):
    return jax.shard_map(
        per_device,
        mesh=mesh,
        in_specs=(P("blk", None, None), P("blk", None)),
        out_specs=P("blk", None),
        check_vma=False,
    )
```

profile of v0, /device:TPU:32, one launch (start us, length us, event | category | flops | bytes accessed | tf_op | source)
XLA Modules:
  0.0 307.8 jit_solution(12379904869405628747)
XLA Ops:
  0.0 0.0 copy-start
  0.0 5.6 %multiply_reduce_fusion = f32[3,1024]{1,0:T(4,128)S(1)} fusion(f32[3,1024,1024]{2,1,0:T(8,128)} %param.4), kind=kLoop, calls=%fused_computation.10 | loop fusion | flops 6288384 | bytes 12595200 | tf_op jit(solution)/shard_map/reduce_sum | solution.py:19
  5.6 0.0 copy-start.1
  5.7 2.5 copy-done
  8.2 3.7 %divide_convert_fusion = bf16[3,1024,1024]{2,1,0:T(8,128)(2,1)} fusion(f32[3,1024,1024]{2,1,0:T(8,128)S(1)} %copy-done, f32[3,1024]{1,0:T(4,128)S(1)} %add_sqrt_fusion), kind=kLoop, calls=%fused_computation.9 | loop fusion | flops 6291456 | bytes 18886656 | tf_op jit(solution)/shard_map/convert_element_type | solution.py:20
  11.9 3.6 %collective-permute-start = (bf16[3,1024,1024]{2,1,0:T(8,128)(2,1)}, bf16[3,1024,1024]{2,1,0:T(8,128)(2,1)}, u32[]{:S(2)}, u32[]{:S(2)}) collective-permute-start(bf16[3,1024,1024]{2,1,0:T(8,128)(2,1)} %divide_convert_fusion), channel_id=1, source_target_pairs={{4,0},{8,4},{12,8},{16,12},{20,16},{24,20},{28,24},{32,28},{36,32}... | collective-permute-start | bytes 18874376 | tf_op jit(solution)/shard_map/ppermute | solution.py:10
  15.5 2.7 collective-permute-start.1
  18.3 0.0 copy-done.1
  18.3 0.7 convert_reduce_fusion
  19.0 0.1 eq.28
  19.1 1.7 sort.17
  20.8 128.9 %collective-permute-done = bf16[3,1024,1024]{2,1,0:T(8,128)(2,1)} collective-permute-done((bf16[3,1024,1024]{2,1,0:T(8,128)(2,1)}, bf16[3,1024,1024]{2,1,0:T(8,128)(2,1)}, u32[]{:S(2)}, u32[]{:S(2)}) %collective-permute-start) | collective-permute-done | bytes 6291488 | tf_op jit(solution)/shard_map/ppermute | solution.py:10
  149.7 69.7 %collective-permute-done.1 = bf16[3,1024,1024]{2,1,0:T(8,128)(2,1)} collective-permute-done((bf16[3,1024,1024]{2,1,0:T(8,128)(2,1)}, bf16[3,1024,1024]{2,1,0:T(8,128)(2,1)}, u32[]{:S(2)}, u32[]{:S(2)}) %collective-permute-start.1) | collective-permute-done | bytes 6291488 | tf_op jit(solution)/shard_map/ppermute | solution.py:10
  219.4 16.3 %pad_maximum_fusion = bf16[9,1024,1024]{2,1,0:T(8,128)(2,1)} fusion(bf16[3,1024,1024]{2,1,0:T(8,128)(2,1)} %collective-permute-done.1, bf16[3,1024,1024]{2,1,0:T(8,128)(2,1)} %collective-permute-done, bf16[3,1024,1024]{2,1,0:T(8,128)(2,1)} %divide_convert_fusion), kind=kLoop, calls=%fused_computation.8 | loop fusion | flops 18874368 | bytes 37748736 | tf_op jit(solution)/shard_map/concatenate | solution.py:25
  235.7 24.8 %while.12 = (s32[]{:T(128)}, f32[9,1024]{1,0:T(8,128)S(1)}, s32[]{:T(128)}, s32[18]{0:T(128)S(1)}, bf16[9,1024,1024]{2,1,0:T(8,128)(2,1)}, /*index=5*/s32[]{:T(1...) while((s32[]{:T(128)}, f32[9,1024]{1,0:T(8,128)S(1)}, ...), condition=%wide.region_6.7_spmd, body=%wide.region_3.6_spmd.sunk | while | flops 2149580800 | bytes 4243866 | solution.py:52
  236.3 0.6 dynamic_slice.55
  238.8 4.7 %fusion.16 = (f32[1024]{0:T(1024)S(1)}, f32[1024]{0:T(1024)S(1)}) fusion(bf16[9,1024,1024]{2,1,0:T(8,128)(2,1)} %get-tuple-element.164, s32[]{:T(128)S(6)} %select_n.121, s32[]{:T(128)S(6)} %select_n.122), kind=kOutput, calls=%fused_computation.32.clone.1 | convolution fusion | flops 2149578752 | bytes 4202504 | tf_op jit(solution)/shard_map/while/body/dot_general | solution.py:40
  243.5 0.1 dynamic_update_slice.15
  243.6 0.1 dynamic_update_slice.16
  244.4 0.6 dynamic_slice.55
  246.8 4.7 %fusion.16 = (f32[1024]{0:T(1024)S(1)}, f32[1024]{0:T(1024)S(1)}) fusion(bf16[9,1024,1024]{2,1,0:T(8,128)(2,1)} %get-tuple-element.164, s32[]{:T(128)S(6)} %select_n.121, s32[]{:T(128)S(6)} %select_n.122), kind=kOutput, calls=%fused_computation.32.clone.1 | convolution fusion | flops 2149578752 | bytes 4202504 | tf_op jit(solution)/shard_map/while/body/dot_general | solution.py:40
  251.5 0.1 dynamic_update_slice.15
  251.7 0.1 dynamic_update_slice.16
  252.4 0.6 dynamic_slice.55
  254.9 4.7 %fusion.16 = (f32[1024]{0:T(1024)S(1)}, f32[1024]{0:T(1024)S(1)}) fusion(bf16[9,1024,1024]{2,1,0:T(8,128)(2,1)} %get-tuple-element.164, s32[]{:T(128)S(6)} %select_n.121, s32[]{:T(128)S(6)} %select_n.122), kind=kOutput, calls=%fused_computation.32.clone.1 | convolution fusion | flops 2149578752 | bytes 4202504 | tf_op jit(solution)/shard_map/while/body/dot_general | solution.py:40
  259.6 0.1 dynamic_update_slice.15
  259.8 0.1 dynamic_update_slice.16
  260.5 1.9 collective-permute-start.2
  262.5 19.5 %collective-permute-start.3 = (f32[3,1024]{1,0:T(4,128)S(1)}, f32[3,1024]{1,0:T(4,128)S(1)}, u32[]{:S(2)}, u32[]{:S(2)}) collective-permute-start(f32[3,1024]{1,0:T(4,128)S(1)} %get-tuple-element.95), channel_id=1, source_target_pairs={{0,8},{4,12},{8,16},{12,20},{16,24},{20,28},{24,32},{28,36},{32,40... | collective-permute-start | bytes 36872 | tf_op jit(solution)/shard_map/ppermute | solution.py:10
  282.0 0.0 collective-permute-done.2
  282.0 1.4 collective-permute-done.3
  283.4 24.4 %pmax.7 = f32[3,1024]{1,0:T(4,128)} all-reduce(f32[3,1024]{1,0:T(4,128)S(1)} %select_maximum_fusion), channel_id=1, replica_groups=mesh['blk'=64,'rep'=4] {'rep'}, use_global_device_ids=true, to_apply=%region_7.8 | all-reduce | flops 3072 | bytes 24576 | tf_op jit(solution)/shard_map/pmax | solution.py:58
  (12 shorter events, 0.2 us)
Async XLA Ops:
  0.0 8.2 %copy-start = (f32[3,1024,1024]{2,1,0:T(8,128)S(1)}, f32[3,1024,1024]{2,1,0:T(8,128)}, u32[]{:S(2)}) copy-start(f32[3,1024,1024]{2,1,0:T(8,128)} %param.4) | copy-start | bytes 37748740
  5.6 12.7 %copy-start.1 = (s32[3,6]{1,0:T(4,128)S(1)}, s32[3,6]{1,0:T(4,128)}, u32[]{:S(2)}) copy-start(s32[3,6]{1,0:T(4,128)} %param.5) | copy-start | bytes 220
  11.9 137.8 %collective-permute-start = (bf16[3,1024,1024]{2,1,0:T(8,128)(2,1)}, bf16[3,1024,1024]{2,1,0:T(8,128)(2,1)}, u32[]{:S(2)}, u32[]{:S(2)}) collective-permute-start(bf16[3,1024,1024]{2,1,0:T(8,128)(2,1)} %divide_convert_fusion), channel_id=1, source_target_pairs={{4,0},{8,4},{12,8},{16,12},{20,16},{24,20},{28,24},{32,28},{36,32}... | collective-permute-start | bytes 18874376 | tf_op jit(solution)/shard_map/ppermute | solution.py:10
  15.5 203.8 %collective-permute-start.1 = (bf16[3,1024,1024]{2,1,0:T(8,128)(2,1)}, bf16[3,1024,1024]{2,1,0:T(8,128)(2,1)}, u32[]{:S(2)}, u32[]{:S(2)}) collective-permute-start(bf16[3,1024,1024]{2,1,0:T(8,128)(2,1)} %divide_convert_fusion), channel_id=1, source_target_pairs={{8,0},{12,4},{16,8},{20,12},{24,16},{28,20},{32,24},{36,28},{40,32... | collective-permute-start | bytes 18874376 | tf_op jit(solution)/shard_map/ppermute | solution.py:10
  260.5 21.5 %collective-permute-start.2 = (f32[3,1024]{1,0:T(4,128)S(1)}, f32[3,1024]{1,0:T(4,128)S(1)}, u32[]{:S(2)}, u32[]{:S(2)}) collective-permute-start(f32[3,1024]{1,0:T(4,128)S(1)} %get-tuple-element.94), channel_id=1, source_target_pairs={{0,4},{4,8},{8,12},{12,16},{16,20},{20,24},{24,28},{28,32},{32,36}... | collective-permute-start | bytes 36872 | tf_op jit(solution)/shard_map/ppermute | solution.py:10
  262.5 21.0 %collective-permute-start.3 = (f32[3,1024]{1,0:T(4,128)S(1)}, f32[3,1024]{1,0:T(4,128)S(1)}, u32[]{:S(2)}, u32[]{:S(2)}) collective-permute-start(f32[3,1024]{1,0:T(4,128)S(1)} %get-tuple-element.95), channel_id=1, source_target_pairs={{0,8},{4,12},{8,16},{12,20},{16,24},{20,28},{24,32},{28,36},{32,40... | collective-permute-start | bytes 36872 | tf_op jit(solution)/shard_map/ppermute | solution.py:10
where the time goes:
time: 310 us; the launch traced here: 308 us
  waiting for transfers between devices  200 us (65%)
  other arithmetic  28.1 us (9%)
  starting transfers between devices  27.8 us (9%)
  blocking collectives  24.4 us (8%)
  matrix products  14 us (5%)
  loops' own time  8.3 us (3%)
  local copies, waits for them, and re-layouts  5.04 us (2%)
    ppermute x4, waiting for transfers between devices, from_behind(): return lax.ppermute(block, axis, route)  200 us
    ppermute x4, starting transfers between devices, from_behind(): return lax.ppermute(block, axis, route)  27.8 us
    pmax x1, blocking collectives, per_device(): return lax.pmax(gathered_best, 'rep')  24.4 us
    concatenate x1, other arithmetic, per_device(): window = jnp.concatenate(pieces, axis=0)  16.3 us
    dot_general x3, matrix products, visit(): lax.dot_general(left, right, (((1,), (1,)), ((), ())), preferred_element_...  14 us
    another operation x1, loops' own time, per_device(): maxima = lax.fori_loop(0, count, visit, start)  8.3 us
  transfers between devices with their start and end apart: 4, of which 3 were waited for; matrix products, arithmetic and copies ran while one was open for 1% of the time, Pallas kernels for 0%

commit v1 on v0

v1 whole, which is shorter than its diff:
```python
import jax
import jax.numpy as jnp
from jax import lax
from jax.experimental import pallas as pl
from jax.experimental.pallas import tpu as pltpu
from jax.sharding import PartitionSpec as P

MESH = pl.DeviceIdType.MESH
REP = 4
PIECES = 4
LANES = 256
NT = (((1,), (1,)), ((), ()))


def fold_lanes(sim):
    out = sim[:, :128]
    for j in range(1, sim.shape[1] // 128):
        out = jnp.maximum(out, sim[:, 128 * j : 128 * (j + 1)])
    return out


def fold_rows(sim):
    return jnp.max(sim.reshape(-1, 8, sim.shape[1]), axis=0)


def kernel(
    places,
    emb,
    pairs,
    out,
    stage,
    own,
    mine,
    near,
    far,
    row_max,
    pairs_here,
    pairs_there,
    pairs_far,
    pairs_far_s,
    msg_row,
    msg_near,
    msg_far,
    got_row,
    got_near,
    got_far,
    load_sem,
    pair_sem,
    far_send,
    far_recv,
    near_send,
    near_recv,
    end_send,
    row_recv,
    got_near_recv,
    got_far_recv,
):
    blocks, rows, width = own.shape
    quarter = rows // REP
    piece = quarter // PIECES
    count = blocks * PIECES
    place = lax.axis_index("blk")
    y = lax.axis_index("rep")
    core = lax.rem(place, 2)
    first = core == 0

    def phys(o):
        return jnp.where(first, o, blocks - 1 - o)

    def at(distance):
        return lax.rem(place + distance + places, places)

    sibling = place + 1 - 2 * core
    sends_to = jnp.where(first, at(-2), at(2))
    gets_from = jnp.where(first, at(2), at(-2))

    def piece_rows(i):
        return pl.ds(pl.multiple_of(y * quarter + (i % PIECES) * piece, piece), piece)

    loads = []
    for i in range(count):
        o = i // PIECES
        loads.append(
            pltpu.make_async_copy(
                emb.at[phys(o), piece_rows(i), :],
                stage.at[o, piece_rows(i), :],
                load_sem.at[i],
            )
        )
    rest = []
    for j in range(1, REP):
        span = pl.ds(pl.multiple_of(lax.rem(y + j, REP) * quarter, quarter), quarter)
        for o in range(blocks):
            rest.append((o, span))
            loads.append(
                pltpu.make_async_copy(
                    emb.at[phys(o), span, :],
                    stage.at[o, span, :],
                    load_sem.at[count + len(rest) - 1],
                )
            )
    for load in loads:
        load.start()
    pairs_load = pltpu.make_async_copy(pairs, pairs_there, pair_sem.at[0])
    pairs_load.start()
    pairs_load_s = pltpu.make_async_copy(pairs, pairs_here, pair_sem.at[1])
    pairs_load_s.start()

    barrier = pltpu.get_barrier_semaphore()
    others = [{"rep": lax.rem(y + j, REP)} for j in range(1, REP)]
    others += [
        {"blk": at(d), "rep": lax.rem(y + j, REP)}
        for d in (-2, 2, -1, 1)
        for j in range(REP)
    ]
    for other in others:
        pl.semaphore_signal(barrier, inc=1, device_id=other, device_id_type=MESH)
    row_max[...] = jnp.full(row_max.shape, -1.0, jnp.float32)
    pl.semaphore_wait(barrier, len(others))

    def unit(block):
        squares = jnp.sum(block * block, axis=1, keepdims=True)
        return (block * lax.rsqrt(squares + 1e-06)).astype(jnp.bfloat16)

    def part(i):
        return pl.ds((i % PIECES) * piece, piece)

    def far_copy(i):
        return pltpu.make_async_remote_copy(
            src_ref=mine.at[i // PIECES, part(i), :],
            dst_ref=far.at[i // PIECES, part(i), :],
            send_sem=far_send.at[i],
            recv_sem=far_recv.at[i],
            device_id={"blk": sends_to},
            device_id_type=MESH,
        )

    def near_copy(i, source):
        return pltpu.make_async_remote_copy(
            src_ref=source.at[i // PIECES, part(i), :],
            dst_ref=near.at[i // PIECES, part(i), :],
            send_sem=near_send.at[i],
            recv_sem=near_recv.at[i],
            device_id={"blk": sibling},
            device_id_type=MESH,
        )

    for i in range(count):
        o = i // PIECES
        loads[i].wait()
        value = unit(stage[o, piece_rows(i), :])
        mine[o, part(i), :] = value
        own[o, piece_rows(i), :] = value
        far_copy(i).start()

        @pl.when(core == 1)
        def _():
            near_copy(i, mine).start()

    pairs_load.wait()
    pairs_load_s.wait()
    pairs_copy = pltpu.make_async_remote_copy(
        src_ref=pairs_there,
        dst_ref=pairs_far,
        send_sem=pair_sem.at[2],
        recv_sem=pair_sem.at[3],
        device_id={"blk": at(2)},
        device_id_type=MESH,
    )
    pairs_copy.start()
    for n, (o, span) in enumerate(rest):
        loads[count + n].wait()
        own[o, span, :] = unit(stage[o, span, :])

    pairs_copy.wait()
    pairs_move = pltpu.make_async_copy(pairs_far, pairs_far_s, pair_sem.at[4])
    pairs_move.start()
    pairs_move.wait()

    def cap(listed):
        return listed.astype(jnp.float32) * 1e30 - 1.0

    def own_cap(o1, o2):
        return cap(pairs_here[jnp.where(first, o1, blocks - 1 - o2), o2 - o1 - 1])

    def near_cap(o, q):
        return cap(
            pairs_here[
                jnp.where(first, o, blocks - 1 - o),
                jnp.where(first, 2 * blocks - 2 - q - o, o + q),
            ]
        )

    def far_cap(o, q):
        here = pairs_here[o, 2 * blocks - 1 + q - o]
        there = pairs_far_s[blocks - 1 - q, 2 * blocks - 1 + q - o]
        return cap(jnp.where(first, here, there))

    def multiply(left, targets):
        kept = None
        for o, limit in targets:
            mine_max = None
            for c in range(rows // LANES):
                lanes = pl.ds(c * LANES, LANES)
                sim = lax.dot_general(
                    left, own[o, lanes, :], NT, preferred_element_type=jnp.float32
                )
                down = jnp.minimum(fold_rows(sim), limit)
                row_max[o, :, lanes] = jnp.maximum(row_max[o, :, lanes], down)
                across = fold_lanes(sim)
                mine_max = across if mine_max is None else jnp.maximum(mine_max, across)
            mine_max = jnp.minimum(mine_max, limit)
            kept = mine_max if kept is None else jnp.maximum(kept, mine_max)
        turned = [
            jnp.max(kept[128 * j : 128 * (j + 1), :].T, axis=0, keepdims=True)
            for j in range(quarter // 128)
        ]
        return jnp.concatenate(turned, axis=1)

    msg_row[...] = jnp.full(msg_row.shape, -1.0, jnp.float32)
    lanes_here = pl.ds(pl.multiple_of(y * quarter, quarter), quarter)
    for q in range(blocks - 1):
        targets = [(o, own_cap(q, o)) for o in range(q + 1, blocks)]
        msg_row[q, :, lanes_here] = multiply(mine[q], targets)

    def near_tiles(q):
        targets = [(o, near_cap(o, q)) for o in range(blocks)]
        msg_near[q] = multiply(near[q], targets)

    def far_tiles(q):
        targets = [(o, far_cap(o, q)) for o in range(q, blocks)]
        msg_far[q] = multiply(far[q], targets)

    @pl.when(core == 0)
    def _():
        def relay(i):
            far_copy(i).wait_recv()
            near_copy(i, far).start()

        half = PIECES // 2
        for q in range(blocks):
            for i in range(half):
                relay(q * PIECES + i)
            for i in range(PIECES):
                near_copy(q * PIECES + i, far).wait_recv()
            near_tiles(q)
            for i in range(half, PIECES):
                relay(q * PIECES + i)
            far_tiles(q)

    @pl.when(core == 1)
    def _():
        for q in range(blocks):
            for i in range(PIECES):
                far_copy(q * PIECES + i).wait_recv()
            far_tiles(q)
            for i in range(PIECES):
                near_copy(q * PIECES + i, mine).wait_recv()
            near_tiles(q)

    for o in range(blocks):
        msg_row[o] = jnp.maximum(msg_row[o], jnp.max(row_max[o], axis=0, keepdims=True))

    def end_copy(k, source, target, recv, blk, rep):
        return pltpu.make_async_remote_copy(
            src_ref=source,
            dst_ref=target.at[y],
            send_sem=end_send.at[k],
            recv_sem=recv.at[y],
            device_id={"blk": blk, "rep": rep},
            device_id_type=MESH,
        )

    ends = []
    for j in range(REP):
        rep = lax.rem(y + j, REP)
        ends.append(end_copy(3 * j, msg_near, got_near, got_near_recv, at(1), rep))
        ends.append(end_copy(3 * j + 1, msg_far, got_far, got_far_recv, gets_from, rep))
        if j:
            ends.append(end_copy(3 * j + 2, msg_row, got_row, row_recv, place, rep))
    for copy in ends:
        copy.start()

    def arrived(source, target, recv, slot):
        pltpu.make_async_remote_copy(
            src_ref=source,
            dst_ref=target.at[slot],
            send_sem=end_send.at[0],
            recv_sem=recv.at[slot],
            device_id={"blk": place, "rep": lax.rem(y + 1, REP)},
            device_id_type=MESH,
        ).wait_recv()

    for j in range(REP):
        slot = lax.rem(y + j, REP)
        arrived(msg_near, got_near, got_near_recv, slot)
        arrived(msg_far, got_far, got_far_recv, slot)
        if j:
            arrived(msg_row, got_row, row_recv, slot)

    best = []
    for o in range(blocks):
        value = msg_row[o]
        for j in range(1, REP):
            value = jnp.maximum(value, got_row[lax.rem(y + j, REP), o])
        side = [jnp.maximum(got_near[j, o], got_far[j, o]) for j in range(REP)]
        best.append(jnp.maximum(value, jnp.concatenate(side, axis=1)))
    for o in range(blocks):
        out[o : o + 1, :] = jnp.where(first, best[o], best[blocks - 1 - o])

    for copy in ends:
        copy.wait_send()
    for i in range(count):
        far_copy(i).wait_send()
        near_copy(i, mine).wait_send()


def solution(mesh):
    places = mesh.shape["blk"]

    def per_device(embeddings, pairs):
        blocks, rows, width = embeddings.shape
        reach = pairs.shape[1]
        quarter = rows // REP
        count = blocks * PIECES
        dma = pltpu.SemaphoreType.DMA

        def body(*refs):
            kernel(places, *refs)

        return pl.pallas_call(
            body,
            out_shape=jax.ShapeDtypeStruct((blocks, rows), jnp.float32),
            in_specs=[pl.BlockSpec(memory_space=pltpu.HBM)] * 2,
            out_specs=pl.BlockSpec(memory_space=pltpu.VMEM),
            scratch_shapes=[
                pltpu.VMEM((blocks, rows, width), jnp.float32),
                pltpu.VMEM((blocks, rows, width), jnp.bfloat16),
                pltpu.VMEM((blocks, quarter, width), jnp.bfloat16),
                pltpu.VMEM((blocks, quarter, width), jnp.bfloat16),
                pltpu.VMEM((blocks, quarter, width), jnp.bfloat16),
                pltpu.VMEM((blocks, 8, rows), jnp.float32),
                pltpu.SMEM((blocks, reach), jnp.int32),
                pltpu.VMEM((blocks, reach), jnp.int32),
                pltpu.VMEM((blocks, reach), jnp.int32),
                pltpu.SMEM((blocks, reach), jnp.int32),
                pltpu.VMEM((blocks, 1, rows), jnp.float32),
                pltpu.VMEM((blocks, 1, quarter), jnp.float32),
                pltpu.VMEM((blocks, 1, quarter), jnp.float32),
                pltpu.VMEM((REP, blocks, 1, rows), jnp.float32),
                pltpu.VMEM((REP, blocks, 1, quarter), jnp.float32),
                pltpu.VMEM((REP, blocks, 1, quarter), jnp.float32),
                dma((count + (REP - 1) * blocks,)),
                dma((5,)),
                dma((count,)),
                dma((count,)),
                dma((count,)),
                dma((count,)),
                dma((3 * REP,)),
                dma((REP,)),
                dma((REP,)),
                dma((REP,)),
            ],
            compiler_params=pltpu.CompilerParams(
                collective_id=0, has_side_effects=True, vmem_limit_bytes=56 << 20
            ),
            name="neighbours",
        )(embeddings, pairs)

    return jax.shard_map(
        per_device,
        mesh=mesh,
        in_specs=(P("blk", None, None), P("blk", None)),
        out_specs=P("blk", None),
        check_vma=False,
    )
```

time: 310 us -> 48.7 us (0.16)
  the two profiles are of different devices: /device:TPU:32 before, /device:TPU:1 now
where the time goes in v1:
time: 48.7 us; the launch traced here: 48.5 us
  Pallas kernels  47.2 us (97%)
  local copies, waits for them, and re-layouts  1.33 us (3%)
    pallas_call x1, Pallas kernels, per_device(): pl.pallas_call(body, out_shape=jax.ShapeDtypeStruct((blocks, rows), jnp.f...  47.2 us
    unnamed x1, local copies, waits for them, and re-layouts  1.33 us

profile of v1, /device:TPU:1, one launch (start us, length us, event | category | flops | bytes accessed | tf_op | source)
XLA Modules:
  0.0 48.5 jit_solution(14689981840036747957)
XLA Ops:
  0.0 47.2 %neighbours.1 = f32[3,1024]{1,0:T(4,128)} custom-call(f32[3,1024,1024]{2,1,0:T(8,128)} %refs_0_.1, s32[3,6]{1,0:T(4,128)} %refs_1_.1), custom_call_target="tpu_custom_call" | custom-call | tf_op jit(solution)/shard_map/neighbours/pallas_call | solution.py:331
  47.2 1.3 %copy.4 = f32[3,1024]{1,0:T(4,128)} copy(f32[3,1024]{1,0:T(4,128)} %neighbours.1) | data formatting | bytes 24576

commit v2 on v1

--- a/solution.py
+++ b/solution.py
@@ -54,6 +54,7 @@
     row_recv,
     got_near_recv,
     got_far_recv,
+    group_sem,
 ):
     blocks, rows, width = own.shape
     quarter = rows // REP
@@ -67,12 +68,15 @@
     def phys(o):
         return jnp.where(first, o, blocks - 1 - o)
 
-    def at(distance):
-        return lax.rem(place + distance + places, places)
+    def within(distance):
+        return jnp.logical_and(place + distance >= 0, place + distance < places)
 
     sibling = place + 1 - 2 * core
-    sends_to = jnp.where(first, at(-2), at(2))
-    gets_from = jnp.where(first, at(2), at(-2))
+    forth = jnp.where(first, -2, 2)
+    sends_to = place + forth
+    gets_from = place - forth
+    sends, gets = within(forth), within(-forth)
+    gets_near = within(1)
 
     def piece_rows(i):
         return pl.ds(pl.multiple_of(y * quarter + (i % PIECES) * piece, piece), piece)
@@ -99,24 +103,42 @@
                     load_sem.at[count + len(rest) - 1],
                 )
             )
+    pairs_load = pltpu.make_async_copy(pairs, pairs_there, pair_sem.at[0])
+    pairs_load.start()
     for load in loads:
         load.start()
-    pairs_load = pltpu.make_async_copy(pairs, pairs_there, pair_sem.at[0])
-    pairs_load.start()
     pairs_load_s = pltpu.make_async_copy(pairs, pairs_here, pair_sem.at[1])
     pairs_load_s.start()
 
+    row_max[...] = jnp.full(row_max.shape, -1.0, jnp.float32)
+    msg_row[...] = jnp.full(msg_row.shape, -1.0, jnp.float32)
+    got_near[...] = jnp.full(got_near.shape, -1.0, jnp.float32)
+    got_far[...] = jnp.full(got_far.shape, -1.0, jnp.float32)
+    pairs_far[...] = jnp.zeros(pairs_far.shape, jnp.int32)
+
     barrier = pltpu.get_barrier_semaphore()
-    others = [{"rep": lax.rem(y + j, REP)} for j in range(1, REP)]
-    others += [
-        {"blk": at(d), "rep": lax.rem(y + j, REP)}
-        for d in (-2, 2, -1, 1)
-        for j in range(REP)
-    ]
-    for other in others:
-        pl.semaphore_signal(barrier, inc=1, device_id=other, device_id_type=MESH)
-    row_max[...] = jnp.full(row_max.shape, -1.0, jnp.float32)
-    pl.semaphore_wait(barrier, len(others))
+    around = (-2, -1, 1, 2)
+    for d in around:
+
+        @pl.when(within(d))
+        def _():
+            pl.semaphore_signal(
+                barrier, inc=1, device_id={"blk": place + d}, device_id_type=MESH
+            )
+
+    for j in range(1, REP):
+        pl.semaphore_signal(
+            barrier, inc=1, device_id={"rep": lax.rem(y + j, REP)}, device_id_type=MESH
+        )
+    neighbours = sum(within(d).astype(jnp.int32) for d in around)
+    pl.semaphore_wait(barrier, neighbours + REP - 1)
+    for d in around:
+
+        @pl.when(within(d))
+        def _():
+            pl.semaphore_signal(
+                group_sem, inc=1, device_id={"blk": place + d}, device_id_type=MESH
+            )
 
     def unit(block):
         squares = jnp.sum(block * block, axis=1, keepdims=True)
@@ -145,36 +167,46 @@
             device_id_type=MESH,
         )
 
+    pairs_load.wait()
+    pairs_copy = pltpu.make_async_remote_copy(
+        src_ref=pairs_there,
+        dst_ref=pairs_far,
+        send_sem=pair_sem.at[2],
+        recv_sem=pair_sem.at[3],
+        device_id={"blk": place + 2},
+        device_id_type=MESH,
+    )
+
+    @pl.when(within(2))
+    def _():
+        pairs_copy.start()
+
     for i in range(count):
         o = i // PIECES
         loads[i].wait()
         value = unit(stage[o, piece_rows(i), :])
         mine[o, part(i), :] = value
         own[o, piece_rows(i), :] = value
-        far_copy(i).start()
+
+        @pl.when(sends)
+        def _():
+            far_copy(i).start()
 
         @pl.when(core == 1)
         def _():
             near_copy(i, mine).start()
 
-    pairs_load.wait()
-    pairs_load_s.wait()
-    pairs_copy = pltpu.make_async_remote_copy(
-        src_ref=pairs_there,
-        dst_ref=pairs_far,
-        send_sem=pair_sem.at[2],
-        recv_sem=pair_sem.at[3],
-        device_id={"blk": at(2)},
-        device_id_type=MESH,
-    )
-    pairs_copy.start()
     for n, (o, span) in enumerate(rest):
         loads[count + n].wait()
         own[o, span, :] = unit(stage[o, span, :])
 
-    pairs_copy.wait()
+    @pl.when(within(-2))
+    def _():
+        pairs_copy.wait_recv()
+
     pairs_move = pltpu.make_async_copy(pairs_far, pairs_far_s, pair_sem.at[4])
     pairs_move.start()
+    pairs_load_s.wait()
     pairs_move.wait()
 
     def cap(listed):
@@ -217,7 +249,6 @@
         ]
         return jnp.concatenate(turned, axis=1)
 
-    msg_row[...] = jnp.full(msg_row.shape, -1.0, jnp.float32)
     lanes_here = pl.ds(pl.multiple_of(y * quarter, quarter), quarter)
     for q in range(blocks - 1):
         targets = [(o, own_cap(q, o)) for o in range(q + 1, blocks)]
@@ -231,32 +262,44 @@
         targets = [(o, far_cap(o, q)) for o in range(q, blocks)]
         msg_far[q] = multiply(far[q], targets)
 
-    @pl.when(core == 0)
-    def _():
-        def relay(i):
-            far_copy(i).wait_recv()
-            near_copy(i, far).start()
-
-        half = PIECES // 2
-        for q in range(blocks):
-            for i in range(half):
-                relay(q * PIECES + i)
-            for i in range(PIECES):
-                near_copy(q * PIECES + i, far).wait_recv()
+    def relay(i):
+        far_copy(i).wait_recv()
+        near_copy(i, far).start()
+
+    half = PIECES // 2
+    for q in range(blocks):
+        pieces = range(q * PIECES, (q + 1) * PIECES)
+
+        @pl.when(core == 0)
+        def _():
+            @pl.when(gets)
+            def _():
+                for i in pieces[:half]:
+                    relay(i)
+
+            for i in pieces:
+                near_copy(i, mine).wait_recv()
             near_tiles(q)
-            for i in range(half, PIECES):
-                relay(q * PIECES + i)
-            far_tiles(q)
-
-    @pl.when(core == 1)
-    def _():
-        for q in range(blocks):
-            for i in range(PIECES):
-                far_copy(q * PIECES + i).wait_recv()
-            far_tiles(q)
-            for i in range(PIECES):
-                near_copy(q * PIECES + i, mine).wait_recv()
-            near_tiles(q)
+
+            @pl.when(gets)
+            def _():
+                for i in pieces[half:]:
+                    relay(i)
+                far_tiles(q)
+
+        @pl.when(core == 1)
+        def _():
+            @pl.when(gets)
+            def _():
+                for i in pieces:
+                    far_copy(i).wait_recv()
+                far_tiles(q)
+
+            @pl.when(gets_near)
+            def _():
+                for i in pieces:
+                    near_copy(i, mine).wait_recv()
+                near_tiles(q)
 
     for o in range(blocks):
         msg_row[o] = jnp.maximum(msg_row[o], jnp.max(row_max[o], axis=0, keepdims=True))
@@ -271,15 +314,35 @@
             device_id_type=MESH,
         )
 
-    ends = []
+    near_ends, far_ends, row_ends = [], [], []
     for j in range(REP):
         rep = lax.rem(y + j, REP)
-        ends.append(end_copy(3 * j, msg_near, got_near, got_near_recv, at(1), rep))
-        ends.append(end_copy(3 * j + 1, msg_far, got_far, got_far_recv, gets_from, rep))
+        near_ends.append(
+            end_copy(3 * j, msg_near, got_near, got_near_recv, place + 1, rep)
+        )
+        far_ends.append(
+            end_copy(3 * j + 1, msg_far, got_far, got_far_recv, gets_from, rep)
+        )
         if j:
-            ends.append(end_copy(3 * j + 2, msg_row, got_row, row_recv, place, rep))
-    for copy in ends:
-        copy.start()
+            row_ends.append(
+                end_copy(3 * j + 2, msg_row, got_row, row_recv, place, rep)
+            )
+    ends = ((gets_near, near_ends), (gets, far_ends), (None, row_ends))
+
+    def each(act):
+        for condition, copies in ends:
+            if condition is None:
+                for copy in copies:
+                    act(copy)
+            else:
+
+                @pl.when(condition)
+                def _():
+                    for copy in copies:
+                        act(copy)
+
+    pl.semaphore_wait(group_sem, neighbours)
+    each(lambda copy: copy.start())
 
     def arrived(source, target, recv, slot):
         pltpu.make_async_remote_copy(
@@ -287,14 +350,21 @@
             dst_ref=target.at[slot],
             send_sem=end_send.at[0],
             recv_sem=recv.at[slot],
-            device_id={"blk": place, "rep": lax.rem(y + 1, REP)},
+            device_id={"rep": lax.rem(y + 1, REP)},
             device_id_type=MESH,
         ).wait_recv()
 
     for j in range(REP):
         slot = lax.rem(y + j, REP)
-        arrived(msg_near, got_near, got_near_recv, slot)
-        arrived(msg_far, got_far, got_far_recv, slot)
+
+        @pl.when(within(-1))
+        def _():
+            arrived(msg_near, got_near, got_near_recv, slot)
+
+        @pl.when(sends)
+        def _():
+            arrived(msg_far, got_far, got_far_recv, slot)
+
         if j:
             arrived(msg_row, got_row, row_recv, slot)
 
@@ -308,11 +378,21 @@
     for o in range(blocks):
         out[o : o + 1, :] = jnp.where(first, best[o], best[blocks - 1 - o])
 
-    for copy in ends:
-        copy.wait_send()
-    for i in range(count):
-        far_copy(i).wait_send()
-        near_copy(i, mine).wait_send()
+    each(lambda copy: copy.wait_send())
+
+    @pl.when(within(2))
+    def _():
+        pairs_copy.wait_send()
+
+    @pl.when(sends)
+    def _():
+        for i in range(count):
+            far_copy(i).wait_send()
+
+    @pl.when(jnp.logical_or(core == 1, gets))
+    def _():
+        for i in range(count):
+            near_copy(i, mine).wait_send()
 
 
 def solution(mesh):
@@ -360,6 +440,7 @@
                 dma((REP,)),
                 dma((REP,)),
                 dma((REP,)),
+                pltpu.SemaphoreType.REGULAR,
             ],
             compiler_params=pltpu.CompilerParams(
                 collective_id=0, has_side_effects=True, vmem_limit_bytes=56 << 20

time: 48.7 us -> 37.2 us (0.76)
  the two profiles are of different devices: /device:TPU:1 before, /device:TPU:128 now
where the time goes in v2:
time: 37.2 us; the launch traced here: 37.1 us
  Pallas kernels  35.7 us (96%)
  local copies, waits for them, and re-layouts  1.33 us (4%)
    pallas_call x1, Pallas kernels, per_device(): pl.pallas_call(body, out_shape=jax.ShapeDtypeStruct((blocks, rows), jnp.f...  35.7 us
    unnamed x1, local copies, waits for them, and re-layouts  1.33 us

profile of v2, /device:TPU:128, one launch (start us, length us, event | category | flops | bytes accessed | tf_op | source)
XLA Modules:
  0.0 37.1 jit_solution(10509724185942925200)
XLA Ops:
  0.0 35.7 %neighbours.1 = f32[3,1024]{1,0:T(4,128)} custom-call(f32[3,1024,1024]{2,1,0:T(8,128)} %refs_0_.1, s32[3,6]{1,0:T(4,128)} %refs_1_.1), custom_call_target="tpu_custom_call" | custom-call | tf_op jit(solution)/shard_map/neighbours/pallas_call | solution.py:411
  35.8 1.3 %copy.4 = f32[3,1024]{1,0:T(4,128)} copy(f32[3,1024]{1,0:T(4,128)} %neighbours.1) | data formatting | bytes 24576

commit v3 on v2

--- a/solution.py
+++ b/solution.py
@@ -50,6 +50,7 @@
     far_recv,
     near_send,
     near_recv,
+    relay_send,
     end_send,
     row_recv,
     got_near_recv,
@@ -78,6 +79,24 @@
     sends, gets = within(forth), within(-forth)
     gets_near = within(1)
 
+    got_near[...] = jnp.full(got_near.shape, -1.0, jnp.float32)
+    got_far[...] = jnp.full(got_far.shape, -1.0, jnp.float32)
+    pairs_far[...] = jnp.zeros(pairs_far.shape, jnp.int32)
+
+    barrier = pltpu.get_barrier_semaphore()
+    around = (-2, -1, 1, 2)
+    for d in around:
+
+        @pl.when(within(d))
+        def _():
+            pl.semaphore_signal(
+                barrier, inc=1, device_id={"blk": place + d}, device_id_type=MESH
+            )
+
+    for j in range(1, REP):
+        pl.semaphore_signal(
+            barrier, inc=1, device_id={"rep": lax.rem(y + j, REP)}, device_id_type=MESH
+        )
     def piece_rows(i):
         return pl.ds(pl.multiple_of(y * quarter + (i % PIECES) * piece, piece), piece)
 
@@ -105,41 +124,15 @@
             )
     pairs_load = pltpu.make_async_copy(pairs, pairs_there, pair_sem.at[0])
     pairs_load.start()
-    for load in loads:
+    for load in loads[:count]:
         load.start()
     pairs_load_s = pltpu.make_async_copy(pairs, pairs_here, pair_sem.at[1])
     pairs_load_s.start()
 
     row_max[...] = jnp.full(row_max.shape, -1.0, jnp.float32)
     msg_row[...] = jnp.full(msg_row.shape, -1.0, jnp.float32)
-    got_near[...] = jnp.full(got_near.shape, -1.0, jnp.float32)
-    got_far[...] = jnp.full(got_far.shape, -1.0, jnp.float32)
-    pairs_far[...] = jnp.zeros(pairs_far.shape, jnp.int32)
-
-    barrier = pltpu.get_barrier_semaphore()
-    around = (-2, -1, 1, 2)
-    for d in around:
-
-        @pl.when(within(d))
-        def _():
-            pl.semaphore_signal(
-                barrier, inc=1, device_id={"blk": place + d}, device_id_type=MESH
-            )
-
-    for j in range(1, REP):
-        pl.semaphore_signal(
-            barrier, inc=1, device_id={"rep": lax.rem(y + j, REP)}, device_id_type=MESH
-        )
+
     neighbours = sum(within(d).astype(jnp.int32) for d in around)
-    pl.semaphore_wait(barrier, neighbours + REP - 1)
-    for d in around:
-
-        @pl.when(within(d))
-        def _():
-            pl.semaphore_signal(
-                group_sem, inc=1, device_id={"blk": place + d}, device_id_type=MESH
-            )
-
     def unit(block):
         squares = jnp.sum(block * block, axis=1, keepdims=True)
         return (block * lax.rsqrt(squares + 1e-06)).astype(jnp.bfloat16)
@@ -157,17 +150,34 @@
             device_id_type=MESH,
         )
 
-    def near_copy(i, source):
+    def last_copy(i):
+        return pltpu.make_async_remote_copy(
+            src_ref=mine.at[i // PIECES, part(i), :],
+            dst_ref=near.at[i // PIECES, part(i), :],
+            send_sem=far_send.at[i],
+            recv_sem=near_recv.at[i],
+            device_id={"blk": place - 1},
+            device_id_type=MESH,
+        )
+
+    def to_sibling(i, source, target, send, recv):
         return pltpu.make_async_remote_copy(
             src_ref=source.at[i // PIECES, part(i), :],
-            dst_ref=near.at[i // PIECES, part(i), :],
-            send_sem=near_send.at[i],
-            recv_sem=near_recv.at[i],
+            dst_ref=target.at[i // PIECES, part(i), :],
+            send_sem=send.at[i],
+            recv_sem=recv.at[i],
             device_id={"blk": sibling},
             device_id_type=MESH,
         )
 
-    pairs_load.wait()
+    def near_copy(i):
+        return to_sibling(i, mine, near, near_send, near_recv)
+
+    def relay_copy(i):
+        if i < last:
+            return to_sibling(i, far, near, relay_send, near_recv)
+        return to_sibling(i, near, far, relay_send, far_recv)
+
     pairs_copy = pltpu.make_async_remote_copy(
         src_ref=pairs_there,
         dst_ref=pairs_far,
@@ -176,25 +186,51 @@
         device_id={"blk": place + 2},
         device_id_type=MESH,
     )
-
-    @pl.when(within(2))
-    def _():
-        pairs_copy.start()
-
+    last = count - PIECES
     for i in range(count):
         o = i // PIECES
         loads[i].wait()
+        if i == 1:
+            for load in loads[count:]:
+                load.start()
         value = unit(stage[o, piece_rows(i), :])
         mine[o, part(i), :] = value
         own[o, piece_rows(i), :] = value
-
-        @pl.when(sends)
-        def _():
-            far_copy(i).start()
+        if i == 0:
+            pairs_load.wait()
+            pl.semaphore_wait(barrier, neighbours + REP - 1)
+
+            @pl.when(within(2))
+            def _():
+                pairs_copy.start()
+
+        if i < last:
+
+            @pl.when(sends)
+            def _():
+                far_copy(i).start()
+
+        else:
+
+            @pl.when(jnp.logical_and(core == 0, sends))
+            def _():
+                last_copy(i).start()
+
+            @pl.when(jnp.logical_and(core == 1, sends))
+            def _():
+                far_copy(i).start()
 
         @pl.when(core == 1)
         def _():
-            near_copy(i, mine).start()
+            near_copy(i).start()
+
+    for d in around:
+
+        @pl.when(within(d))
+        def _():
+            pl.semaphore_signal(
+                group_sem, inc=1, device_id={"blk": place + d}, device_id_type=MESH
+            )
 
     for n, (o, span) in enumerate(rest):
         loads[count + n].wait()
@@ -262,48 +298,6 @@
         targets = [(o, far_cap(o, q)) for o in range(q, blocks)]
         msg_far[q] = multiply(far[q], targets)
 
-    def relay(i):
-        far_copy(i).wait_recv()
-        near_copy(i, far).start()
-
-    half = PIECES // 2
-    for q in range(blocks):
-        pieces = range(q * PIECES, (q + 1) * PIECES)
-
-        @pl.when(core == 0)
-        def _():
-            @pl.when(gets)
-            def _():
-                for i in pieces[:half]:
-                    relay(i)
-
-            for i in pieces:
-                near_copy(i, mine).wait_recv()
-            near_tiles(q)
-
-            @pl.when(gets)
-            def _():
-                for i in pieces[half:]:
-                    relay(i)
-                far_tiles(q)
-
-        @pl.when(core == 1)
-        def _():
-            @pl.when(gets)
-            def _():
-                for i in pieces:
-                    far_copy(i).wait_recv()
-                far_tiles(q)
-
-            @pl.when(gets_near)
-            def _():
-                for i in pieces:
-                    near_copy(i, mine).wait_recv()
-                near_tiles(q)
-
-    for o in range(blocks):
-        msg_row[o] = jnp.maximum(msg_row[o], jnp.max(row_max[o], axis=0, keepdims=True))
-
     def end_copy(k, source, target, recv, blk, rep):
         return pltpu.make_async_remote_copy(
             src_ref=source,
@@ -316,7 +310,7 @@
 
     near_ends, far_ends, row_ends = [], [], []
     for j in range(REP):
-        rep = lax.rem(y + j, REP)
+        rep = lax.rem(y + REP - j, REP)
         near_ends.append(
             end_copy(3 * j, msg_near, got_near, got_near_recv, place + 1, rep)
         )
@@ -327,22 +321,83 @@
             row_ends.append(
                 end_copy(3 * j + 2, msg_row, got_row, row_recv, place, rep)
             )
-    ends = ((gets_near, near_ends), (gets, far_ends), (None, row_ends))
-
-    def each(act):
-        for condition, copies in ends:
-            if condition is None:
-                for copy in copies:
-                    act(copy)
-            else:
-
-                @pl.when(condition)
-                def _():
-                    for copy in copies:
-                        act(copy)
+
+    def fold(o):
+        msg_row[o] = jnp.maximum(
+            msg_row[o], jnp.max(row_max[o], axis=0, keepdims=True)
+        )
+
+    def relay(i):
+        (far_copy(i) if i < last else near_copy(i)).wait_recv()
+        relay_copy(i).start()
+
+    half = PIECES // 2
+    for q in range(blocks - 1):
+        pieces = range(q * PIECES, (q + 1) * PIECES)
+
+        @pl.when(core == 0)
+        def _():
+            @pl.when(gets)
+            def _():
+                for i in pieces[:half]:
+                    relay(i)
+
+            for i in pieces:
+                near_copy(i).wait_recv()
+            near_tiles(q)
+
+            @pl.when(gets)
+            def _():
+                for i in pieces[half:]:
+                    relay(i)
+                far_tiles(q)
+
+        @pl.when(core == 1)
+        def _():
+            @pl.when(gets)
+            def _():
+                for i in pieces:
+                    far_copy(i).wait_recv()
+                far_tiles(q)
+
+            @pl.when(gets_near)
+            def _():
+                for i in pieces:
+                    near_copy(i).wait_recv()
+                near_tiles(q)
 
     pl.semaphore_wait(group_sem, neighbours)
-    each(lambda copy: copy.start())
+
+    @pl.when(gets_near)
+    def _():
+        @pl.when(core == 0)
+        def _():
+            for i in range(last, count):
+                near_copy(i).wait_recv()
+
+        @pl.when(core == 1)
+        def _():
+            for i in range(last, count):
+                relay(i)
+
+        near_tiles(blocks - 1)
+        for copy in near_ends:
+            copy.start()
+
+    for o in range(blocks - 1):
+        fold(o)
+
+    @pl.when(gets)
+    def _():
+        for i in range(last, count):
+            far_copy(i).wait_recv()
+        far_tiles(blocks - 1)
+        for copy in far_ends:
+            copy.start()
+
+    fold(blocks - 1)
+    for copy in row_ends:
+        copy.start()
 
     def arrived(source, target, recv, slot):
         pltpu.make_async_remote_copy(
@@ -354,19 +409,18 @@
             device_id_type=MESH,
         ).wait_recv()
 
-    for j in range(REP):
-        slot = lax.rem(y + j, REP)
-
-        @pl.when(within(-1))
-        def _():
-            arrived(msg_near, got_near, got_near_recv, slot)
-
-        @pl.when(sends)
-        def _():
-            arrived(msg_far, got_far, got_far_recv, slot)
-
-        if j:
-            arrived(msg_row, got_row, row_recv, slot)
+    @pl.when(within(-1))
+    def _():
+        for j in range(REP):
+            arrived(msg_near, got_near, got_near_recv, lax.rem(y + j, REP))
+
+    @pl.when(sends)
+    def _():
+        for j in range(REP):
+            arrived(msg_far, got_far, got_far_recv, lax.rem(y + j, REP))
+
+    for j in range(1, REP):
+        arrived(msg_row, got_row, row_recv, lax.rem(y + j, REP))
 
     best = []
     for o in range(blocks):
@@ -378,7 +432,18 @@
     for o in range(blocks):
         out[o : o + 1, :] = jnp.where(first, best[o], best[blocks - 1 - o])
 
-    each(lambda copy: copy.wait_send())
+    for copy in row_ends:
+        copy.wait_send()
+
+    @pl.when(gets_near)
+    def _():
+        for copy in near_ends:
+            copy.wait_send()
+
+    @pl.when(gets)
+    def _():
+        for copy in far_ends:
+            copy.wait_send()
 
     @pl.when(within(2))
     def _():
@@ -389,10 +454,20 @@
         for i in range(count):
             far_copy(i).wait_send()
 
-    @pl.when(jnp.logical_or(core == 1, gets))
+    @pl.when(core == 1)
     def _():
         for i in range(count):
-            near_copy(i, mine).wait_send()
+            near_copy(i).wait_send()
+
+        @pl.when(gets_near)
+        def _():
+            for i in range(last, count):
+                relay_copy(i).wait_send()
+
+    @pl.when(jnp.logical_and(core == 0, gets))
+    def _():
+        for i in range(last):
+            relay_copy(i).wait_send()
 
 
 def solution(mesh):
@@ -436,6 +511,7 @@
                 dma((count,)),
                 dma((count,)),
                 dma((count,)),
+                dma((count,)),
                 dma((3 * REP,)),
                 dma((REP,)),
                 dma((REP,)),

time: 37.2 us -> 35 us (0.941)
  Pallas kernels: 35.7 us -> 33.5 us
    pallas_call x1, Pallas kernels: 35.7 us -> 33.5 us  [per_device(): pl.pallas_call(body, out_shape=jax.ShapeDtypeStruct((blocks, rows), jnp.f...]
where the time goes in v3:
time: 35 us; the launch traced here: 34.8 us
  Pallas kernels  33.5 us (96%)
  local copies, waits for them, and re-layouts  1.33 us (4%)
    pallas_call x1, Pallas kernels, per_device(): pl.pallas_call(body, out_shape=jax.ShapeDtypeStruct((blocks, rows), jnp.f...  33.5 us
    unnamed x1, local copies, waits for them, and re-layouts  1.33 us

profile of v3, /device:TPU:128, one launch (start us, length us, event | category | flops | bytes accessed | tf_op | source)
XLA Modules:
  0.0 34.8 jit_solution(8616239789009842013)
XLA Ops:
  0.0 33.5 %neighbours.1 = f32[3,1024]{1,0:T(4,128)} custom-call(f32[3,1024,1024]{2,1,0:T(8,128)} %refs_0_.1, s32[3,6]{1,0:T(4,128)} %refs_1_.1), custom_call_target="tpu_custom_call" | custom-call | tf_op jit(solution)/shard_map/neighbours/pallas_call | solution.py:486
  33.5 1.3 %copy.4 = f32[3,1024]{1,0:T(4,128)} copy(f32[3,1024]{1,0:T(4,128)} %neighbours.1) | data formatting | bytes 24576

commit v4 on v3

--- a/solution.py
+++ b/solution.py
@@ -7,7 +7,7 @@
 
 MESH = pl.DeviceIdType.MESH
 REP = 4
-PIECES = 4
+CUTS = ((2, 2), (2, 2), (2, 4, 4))
 LANES = 256
 NT = (((1,), (1,)), ((), ()))
 
@@ -59,8 +59,13 @@
 ):
     blocks, rows, width = own.shape
     quarter = rows // REP
-    piece = quarter // PIECES
-    count = blocks * PIECES
+    parts = []
+    for o, cut in enumerate(CUTS):
+        start = 0
+        for share in cut:
+            parts.append((o, start, quarter // share))
+            start += quarter // share
+    count = len(parts)
     place = lax.axis_index("blk")
     y = lax.axis_index("rep")
     core = lax.rem(place, 2)
@@ -79,12 +84,8 @@
     sends, gets = within(forth), within(-forth)
     gets_near = within(1)
 
-    got_near[...] = jnp.full(got_near.shape, -1.0, jnp.float32)
-    got_far[...] = jnp.full(got_far.shape, -1.0, jnp.float32)
-    pairs_far[...] = jnp.zeros(pairs_far.shape, jnp.int32)
-
     barrier = pltpu.get_barrier_semaphore()
-    around = (-2, -1, 1, 2)
+    around = (-forth, forth, 1, -1)
     for d in around:
 
         @pl.when(within(d))
@@ -93,16 +94,18 @@
                 barrier, inc=1, device_id={"blk": place + d}, device_id_type=MESH
             )
 
-    for j in range(1, REP):
+    for j in (2, 1, 3):
         pl.semaphore_signal(
             barrier, inc=1, device_id={"rep": lax.rem(y + j, REP)}, device_id_type=MESH
         )
+
     def piece_rows(i):
-        return pl.ds(pl.multiple_of(y * quarter + (i % PIECES) * piece, piece), piece)
+        _, start, size = parts[i]
+        return pl.ds(pl.multiple_of(y * quarter + start, size), size)
 
     loads = []
     for i in range(count):
-        o = i // PIECES
+        o = parts[i][0]
         loads.append(
             pltpu.make_async_copy(
                 emb.at[phys(o), piece_rows(i), :],
@@ -132,18 +135,35 @@
     row_max[...] = jnp.full(row_max.shape, -1.0, jnp.float32)
     msg_row[...] = jnp.full(msg_row.shape, -1.0, jnp.float32)
 
+
+    @pl.when(jnp.logical_not(within(-1)))
+    def _():
+        got_near[...] = jnp.full(got_near.shape, -1.0, jnp.float32)
+
+    @pl.when(jnp.logical_not(sends))
+    def _():
+        got_far[...] = jnp.full(got_far.shape, -1.0, jnp.float32)
+
+    @pl.when(jnp.logical_not(within(-2)))
+    def _():
+        pairs_far[...] = jnp.zeros(pairs_far.shape, jnp.int32)
+
     neighbours = sum(within(d).astype(jnp.int32) for d in around)
     def unit(block):
         squares = jnp.sum(block * block, axis=1, keepdims=True)
         return (block * lax.rsqrt(squares + 1e-06)).astype(jnp.bfloat16)
 
     def part(i):
-        return pl.ds((i % PIECES) * piece, piece)
+        _, start, size = parts[i]
+        return pl.ds(start, size)
+
+    def of_block(q):
+        return [i for i in range(count) if parts[i][0] == q]
 
     def far_copy(i):
         return pltpu.make_async_remote_copy(
-            src_ref=mine.at[i // PIECES, part(i), :],
-            dst_ref=far.at[i // PIECES, part(i), :],
+            src_ref=mine.at[parts[i][0], part(i), :],
+            dst_ref=far.at[parts[i][0], part(i), :],
             send_sem=far_send.at[i],
             recv_sem=far_recv.at[i],
             device_id={"blk": sends_to},
@@ -152,8 +172,8 @@
 
     def last_copy(i):
         return pltpu.make_async_remote_copy(
-            src_ref=mine.at[i // PIECES, part(i), :],
-            dst_ref=near.at[i // PIECES, part(i), :],
+            src_ref=mine.at[parts[i][0], part(i), :],
+            dst_ref=near.at[parts[i][0], part(i), :],
             send_sem=far_send.at[i],
             recv_sem=near_recv.at[i],
             device_id={"blk": place - 1},
@@ -162,8 +182,8 @@
 
     def to_sibling(i, source, target, send, recv):
         return pltpu.make_async_remote_copy(
-            src_ref=source.at[i // PIECES, part(i), :],
-            dst_ref=target.at[i // PIECES, part(i), :],
+            src_ref=source.at[parts[i][0], part(i), :],
+            dst_ref=target.at[parts[i][0], part(i), :],
             send_sem=send.at[i],
             recv_sem=recv.at[i],
             device_id={"blk": sibling},
@@ -186,9 +206,9 @@
         device_id={"blk": place + 2},
         device_id_type=MESH,
     )
-    last = count - PIECES
+    last = of_block(blocks - 1)[0]
     for i in range(count):
-        o = i // PIECES
+        o = parts[i][0]
         loads[i].wait()
         if i == 1:
             for load in loads[count:]:
@@ -309,8 +329,8 @@
         )
 
     near_ends, far_ends, row_ends = [], [], []
-    for j in range(REP):
-        rep = lax.rem(y + REP - j, REP)
+    for j in (2, 1, 3, 0):
+        rep = lax.rem(y + j, REP)
         near_ends.append(
             end_copy(3 * j, msg_near, got_near, got_near_recv, place + 1, rep)
         )
@@ -331,9 +351,9 @@
         (far_copy(i) if i < last else near_copy(i)).wait_recv()
         relay_copy(i).start()
 
-    half = PIECES // 2
     for q in range(blocks - 1):
-        pieces = range(q * PIECES, (q + 1) * PIECES)
+        pieces = of_block(q)
+        half = len(pieces) // 2
 
         @pl.when(core == 0)
         def _():
@@ -477,7 +497,7 @@
         blocks, rows, width = embeddings.shape
         reach = pairs.shape[1]
         quarter = rows // REP
-        count = blocks * PIECES
+        count = sum(len(cut) for cut in CUTS)
         dma = pltpu.SemaphoreType.DMA
 
         def body(*refs):
@@ -485,7 +505,7 @@
 
         return pl.pallas_call(
             body,
-            out_shape=jax.ShapeDtypeStruct((blocks, rows), jnp.float32),
+            out_shape=pltpu.VMEM((blocks, rows), jnp.float32),
             in_specs=[pl.BlockSpec(memory_space=pltpu.HBM)] * 2,
             out_specs=pl.BlockSpec(memory_space=pltpu.VMEM),
             scratch_shapes=[

time: 35 us -> 33.2 us (0.949)
  Pallas kernels: 33.5 us -> 32.5 us
  local copies, waits for them, and re-layouts: 1.33 us -> 0.61 us
    pallas_call x1, Pallas kernels: 33.5 us -> 32.5 us  [per_device(): pl.pallas_call(body, out_shape=pltpu.VMEM((blocks, rows), jnp.float32), i...]
    unnamed x1, local copies, waits for them, and re-layouts: 1.33 us -> 0.61 us
where the time goes in v4:
time: 33.2 us; the launch traced here: 33.1 us
  Pallas kernels  32.5 us (98%)
  local copies, waits for them, and re-layouts  0.61 us (2%)
    pallas_call x1, Pallas kernels, per_device(): pl.pallas_call(body, out_shape=pltpu.VMEM((blocks, rows), jnp.float32), i...  32.5 us

profile of v4, /device:TPU:128, one launch (start us, length us, event | category | flops | bytes accessed | tf_op | source)
XLA Modules:
  0.0 33.1 jit_solution(17708072919576281525)
XLA Ops:
  0.0 32.5 %neighbours.1 = f32[3,1024]{1,0:T(4,128)S(1)} custom-call(f32[3,1024,1024]{2,1,0:T(8,128)} %refs_0_.1, s32[3,6]{1,0:T(4,128)} %refs_1_.1), custom_call_target="tpu_custom_call" | custom-call | tf_op jit(solution)/shard_map/neighbours/pallas_call | solution.py:506
  32.5 0.6 %copy.4 = f32[3,1024]{1,0:T(4,128)} copy(f32[3,1024]{1,0:T(4,128)S(1)} %neighbours.1) | data formatting | bytes 24576

commit v5 on v4

--- a/solution.py
+++ b/solution.py
@@ -7,7 +7,7 @@
 
 MESH = pl.DeviceIdType.MESH
 REP = 4
-CUTS = ((2, 2), (2, 2), (2, 4, 4))
+CUTS = ((1,), (1,), (2, 4, 4))
 LANES = 256
 NT = (((1,), (1,)), ((), ()))
 
@@ -79,8 +79,12 @@
 
     sibling = place + 1 - 2 * core
     forth = jnp.where(first, -2, 2)
-    sends_to = place + forth
-    gets_from = place - forth
+
+    def at(distance):
+        return lax.rem(place + distance + places, places)
+
+    sends_to = at(forth)
+    gets_from = at(-forth)
     sends, gets = within(forth), within(-forth)
     gets_near = within(1)
 
@@ -176,7 +180,7 @@
             dst_ref=near.at[parts[i][0], part(i), :],
             send_sem=far_send.at[i],
             recv_sem=near_recv.at[i],
-            device_id={"blk": place - 1},
+            device_id={"blk": at(-1)},
             device_id_type=MESH,
         )
 
@@ -203,7 +207,7 @@
         dst_ref=pairs_far,
         send_sem=pair_sem.at[2],
         recv_sem=pair_sem.at[3],
-        device_id={"blk": place + 2},
+        device_id={"blk": at(2)},
         device_id_type=MESH,
     )
     last = of_block(blocks - 1)[0]
@@ -332,7 +336,7 @@
     for j in (2, 1, 3, 0):
         rep = lax.rem(y + j, REP)
         near_ends.append(
-            end_copy(3 * j, msg_near, got_near, got_near_recv, place + 1, rep)
+            end_copy(3 * j, msg_near, got_near, got_near_recv, at(1), rep)
         )
         far_ends.append(
             end_copy(3 * j + 1, msg_far, got_far, got_far_recv, gets_from, rep)
@@ -418,6 +422,43 @@
     fold(blocks - 1)
     for copy in row_ends:
         copy.start()
+
+    @pl.when(within(2))
+    def _():
+        pairs_copy.wait_send()
+
+    @pl.when(sends)
+    def _():
+        for i in range(count):
+            far_copy(i).wait_send()
+
+    @pl.when(core == 1)
+    def _():
+        for i in range(count):
+            near_copy(i).wait_send()
+
+        @pl.when(gets_near)
+        def _():
+            for i in range(last, count):
+                relay_copy(i).wait_send()
+
+    @pl.when(jnp.logical_and(core == 0, gets))
+    def _():
+        for i in range(last):
+            relay_copy(i).wait_send()
+
+    for copy in row_ends:
+        copy.wait_send()
+
+    @pl.when(gets_near)
+    def _():
+        for copy in near_ends:
+            copy.wait_send()
+
+    @pl.when(gets)
+    def _():
+        for copy in far_ends:
+            copy.wait_send()
 
     def arrived(source, target, recv, slot):
         pltpu.make_async_remote_copy(
@@ -434,60 +475,26 @@
         for j in range(REP):
             arrived(msg_near, got_near, got_near_recv, lax.rem(y + j, REP))
 
+    best = []
+    for o in range(blocks):
+        side = [got_near[j, o] for j in range(REP)]
+        best.append(jnp.maximum(msg_row[o], jnp.concatenate(side, axis=1)))
+    for j in range(1, REP):
+        arrived(msg_row, got_row, row_recv, lax.rem(y + j, REP))
+    for o in range(blocks):
+        for j in range(1, REP):
+            best[o] = jnp.maximum(best[o], got_row[lax.rem(y + j, REP), o])
+
     @pl.when(sends)
     def _():
         for j in range(REP):
             arrived(msg_far, got_far, got_far_recv, lax.rem(y + j, REP))
 
-    for j in range(1, REP):
-        arrived(msg_row, got_row, row_recv, lax.rem(y + j, REP))
-
-    best = []
     for o in range(blocks):
-        value = msg_row[o]
-        for j in range(1, REP):
-            value = jnp.maximum(value, got_row[lax.rem(y + j, REP), o])
-        side = [jnp.maximum(got_near[j, o], got_far[j, o]) for j in range(REP)]
-        best.append(jnp.maximum(value, jnp.concatenate(side, axis=1)))
+        side = [got_far[j, o] for j in range(REP)]
+        best[o] = jnp.maximum(best[o], jnp.concatenate(side, axis=1))
     for o in range(blocks):
         out[o : o + 1, :] = jnp.where(first, best[o], best[blocks - 1 - o])
-
-    for copy in row_ends:
-        copy.wait_send()
-
-    @pl.when(gets_near)
-    def _():
-        for copy in near_ends:
-            copy.wait_send()
-
-    @pl.when(gets)
-    def _():
-        for copy in far_ends:
-            copy.wait_send()
-
-    @pl.when(within(2))
-    def _():
-        pairs_copy.wait_send()
-
-    @pl.when(sends)
-    def _():
-        for i in range(count):
-            far_copy(i).wait_send()
-
-    @pl.when(core == 1)
-    def _():
-        for i in range(count):
-            near_copy(i).wait_send()
-
-        @pl.when(gets_near)
-        def _():
-            for i in range(last, count):
-                relay_copy(i).wait_send()
-
-    @pl.when(jnp.logical_and(core == 0, gets))
-    def _():
-        for i in range(last):
-            relay_copy(i).wait_send()
 
 
 def solution(mesh):

time: 33.2 us -> 33 us (level)
  no operation moved by 1% of the time
where the time goes in v5:
time: 33 us
  Pallas kernels  32.4 us (98%)
  local copies, waits for them, and re-layouts  0.61 us (2%)
    pallas_call x1, Pallas kernels, per_device(): pl.pallas_call(body, out_shape=pltpu.VMEM((blocks, rows), jnp.float32), i...  32.4 us

profile of v5, /device:TPU:128, one launch (start us, length us, event | category | flops | bytes accessed | tf_op | source)
XLA Modules:
  0.0 33.0 jit_solution(2244106576809171834)
XLA Ops:
  0.0 32.4 %neighbours.1 = f32[3,1024]{1,0:T(4,128)S(1)} custom-call(f32[3,1024,1024]{2,1,0:T(8,128)} %refs_0_.1, s32[3,6]{1,0:T(4,128)} %refs_1_.1), custom_call_target="tpu_custom_call" | custom-call | tf_op jit(solution)/shard_map/neighbours/pallas_call | solution.py:513
  32.4 0.6 %copy.4 = f32[3,1024]{1,0:T(4,128)} copy(f32[3,1024]{1,0:T(4,128)S(1)} %neighbours.1) | data formatting | bytes 24576
